TPU v7x, 32 devices: a whole 2x2x4 slice. The times are simulated.
32 devices in a mesh: dp: 4 (over z), mp: 8 (over y, x, core).
Axes of the slice: x: 2, y: 2, z: 4, core: 2. Of those that a mesh axis runs over, the one named last changes fastest.
Arguments:
- tokens: bfloat16 [8192, 16384], P('dp', 'mp'), may hold values from -6 to 6
- inner_one: bfloat16 [128, 128, 128], P('mp'), may hold values from -0.5 to 0.5
- outer_one: bfloat16 [128, 128, 128], P('mp'), may hold values from -0.5 to 0.5
- inner_two: bfloat16 [128, 128, 128], P('mp'), may hold values from -0.5 to 0.5
- outer_two: bfloat16 [128, 128, 128], P('mp'), may hold values from -0.5 to 0.5
- cotangent: bfloat16 [8192, 16384], P('dp', 'mp'), may hold values from -6 to 6
Outputs:
- output: bfloat16 [8192, 16384], P('dp', 'mp')
- input_grad: bfloat16 [8192, 16384], P('dp', 'mp')
- inner_one_grad: float32 [128, 128, 128], P('mp', 'dp')
- outer_one_grad: float32 [128, 128, 128], P('mp', 'dp')
- inner_two_grad: float32 [128, 128, 128], P('mp', 'dp')
- outer_two_grad: float32 [128, 128, 128], P('mp', 'dp')
All inputs are finite; a program needn't handle non-finite values.
Results may differ from a plain program's by a relative error of at most 0.0069.
Values may be sent and summed in bfloat16 or wider, within the bound.
A program may use at most 192 MiB of HBM per device.

v0:
```python
import jax
import jax.numpy as jnp
from jax import lax
from jax.sharding import PartitionSpec as P


def gelu_tanh(values):
    return jax.nn.gelu(values, approximate=True)


def product(form, left, right):
    return jnp.einsum(form, left, right, preferred_element_type=jnp.float32)


def return_second(grads, outer_two):
    grad_perm_two = product("tjl,jbl->jbt", grads, outer_two).astype(jnp.bfloat16)
    return lax.all_to_all(grad_perm_two, "mp", split_axis=1, concat_axis=0, tiled=True)


def body(tokens, inner_one, outer_one, inner_two, outer_two, cotangent):
    tok_rows = tokens.shape[0]
    local_blocks = inner_one.shape[0]
    block_size = inner_one.shape[1]
    inputs = tokens.reshape(tok_rows, local_blocks, block_size)
    grads = cotangent.reshape(tok_rows, local_blocks, block_size)
    first_mid = product("tbk,bkj->jbt", inputs, inner_one).astype(jnp.bfloat16)
    first_perm = lax.all_to_all(first_mid, "mp", split_axis=0, concat_axis=1, tiled=True)
    pre_act = product("jbt,jbl->tjl", first_perm, outer_one)
    hidden = gelu_tanh(pre_act).astype(jnp.bfloat16)
    second_mid = product("tbk,bkj->jbt", hidden, inner_two).astype(jnp.bfloat16)
    second_perm = lax.all_to_all(second_mid, "mp", split_axis=0, concat_axis=1, tiled=True)
    output = product("jbt,jbl->tjl", second_perm, outer_two).astype(jnp.bfloat16)
    outer_two_grad = product("jbt,tjl->jbl", second_perm, grads)
    outer_two_grad = lax.psum_scatter(outer_two_grad, "dp", scatter_dimension=1, tiled=True)
    grad_mid_two = return_second(grads, outer_two)
    grad_hidden = product("jbt,bkj->tbk", grad_mid_two, inner_two)
    inner_two_grad = product("tbk,jbt->bkj", hidden, grad_mid_two)
    inner_two_grad = lax.psum_scatter(inner_two_grad, "dp", scatter_dimension=1, tiled=True)
    primal_out, pullback = jax.vjp(gelu_tanh, pre_act)
    grad_pre = pullback(grad_hidden)[0].astype(jnp.bfloat16)
    grad_perm_one = product("tjl,jbl->jbt", grad_pre, outer_one).astype(jnp.bfloat16)
    outer_one_grad = product("jbt,tjl->jbl", first_perm, grad_pre)
    outer_one_grad = lax.psum_scatter(outer_one_grad, "dp", scatter_dimension=1, tiled=True)
    grad_mid_one = lax.all_to_all(grad_perm_one, "mp", split_axis=1, concat_axis=0, tiled=True)
    input_grad = product("jbt,bkj->tbk", grad_mid_one, inner_one).astype(jnp.bfloat16)
    inner_one_grad = product("tbk,jbt->bkj", inputs, grad_mid_one)
    inner_one_grad = lax.psum_scatter(inner_one_grad, "dp", scatter_dimension=1, tiled=True)
    width_here = local_blocks * block_size
    return (
        output.reshape(tok_rows, width_here),
        input_grad.reshape(tok_rows, width_here),
        inner_one_grad,
        outer_one_grad,
        inner_two_grad,
        outer_two_grad,
    )


def solution(mesh):
    placed = (
        P("dp", "mp"),
        P("mp", None, None),
        P("mp", None, None),
        P("mp", None, None),
        P("mp", None, None),
        P("dp", "mp"),
    )
    return jax.shard_map(
        body,
        mesh=mesh,
        in_specs=placed,
        out_specs=(
            P("dp", "mp"),
            P("dp", "mp"),
            P("mp", "dp", None),
            P("mp", "dp", None),
            P("mp", "dp", None),
            P("mp", "dp", None),
        ),
        check_vma=False,
    )
```

profile of v0, /device:TPU:0, one launch (start us, length us, event | category | flops | bytes accessed | tf_op | source)
XLA Modules:
  0.0 566.4 jit_solution(4513090994323310125)
XLA Ops:
  7.2 9.5 %convert_bitcast_fusion.2 = bf16[128,16,2048]{2,0,1:T(8,128)(2,1)} fusion(bf16[16,128,128]{2,1,0:T(8,128)(2,1)} %param.7, bf16[2048,2048]{1,0:T(8,128)(2,1)} %param.6), kind=kOutput, calls=%fused_computation.26 | convolution fusion | flops 1077936128 | bytes 17301504 | tf_op jit(solution)/shard_map/tbk,bkj->jbt/dot_general | solution.py:12
  16.6 11.4 %copy.70 = bf16[128,16,2048]{2,1,0:T(8,128)(2,1)} copy(bf16[128,16,2048]{2,0,1:T(8,128)(2,1)} %convert_bitcast_fusion.2) | data formatting | bytes 16777216 | tf_op jit(solution)/shard_map/convert_element_type | solution.py:26
  28.1 5.6 all-to-all-start
  33.6 9.2 %fusion.29 = bf16[16,128,2048]{2,1,0:T(8,128)(2,1)} fusion(bf16[16,128,128]{2,1,0:T(8,128)(2,1)S(1)} %copy-done.3, bf16[2048,2048]{1,0:T(8,128)(2,1)} %param.11), kind=kOutput, calls=%fused_computation.35 | convolution fusion | flops 1077936128 | bytes 17301504 | tf_op jit(solution)/shard_map/tjl,jbl->jbt/dot_general | solution.py:12
  42.9 11.2 %copy.77 = bf16[16,128,2048]{2,0,1:T(8,128)(2,1)} copy(bf16[16,128,2048]{2,1,0:T(8,128)(2,1)} %fusion.29) | data formatting | bytes 16777216 | tf_op jit(solution)/shard_map/convert_element_type | solution.py:16
  54.1 74.0 %all-to-all-done = bf16[128,16,2048]{2,1,0:T(8,128)(2,1)} async-done(((bf16[128,16,2048]{2,1,0:T(8,128)(2,1)}), bf16[128,16,2048]{2,1,0:T(8,128)(2,1)}, u32[]{:S(2)}, u32[]{:S(2)}) %all-to-all-start) | async-done | bytes 8388640 | tf_op jit(solution)/shard_map/all_to_all | solution.py:27
  128.1 5.2 all-to-all-start.2
  133.3 8.4 %copy.71 = bf16[16,8,16,2048]{3,2,1,0:T(8,128)(2,1)} copy(bf16[16,8,16,2048]{3,2,0,1:T(8,128)(2,1)} %bitcast.2) | data formatting | bytes 16777216 | tf_op jit(solution)/shard_map/all_to_all | solution.py:27
  141.7 85.6 %all-to-all-done.2 = bf16[16,128,2048]{2,0,1:T(8,128)(2,1)} async-done(((bf16[16,128,2048]{2,0,1:T(8,128)(2,1)}), bf16[16,128,2048]{2,0,1:T(8,128)(2,1)}, u32[]{:S(2)}, u32[]{:S(2)}) %all-to-all-start.2) | async-done | bytes 8388640 | tf_op jit(solution)/shard_map/all_to_all | solution.py:17
  227.4 12.1 %copy.79 = bf16[8,16,16,2048]{3,2,1,0:T(8,128)(2,1)} copy(bf16[8,16,16,2048]{3,1,2,0:T(8,128)(2,1)} %bitcast.13) | data formatting | bytes 16777216 | tf_op jit(solution)/shard_map/all_to_all | solution.py:17
  239.5 11.7 %fusion.39 = f32[16,2048,128]{2,1,0:T(8,128)} fusion(bf16[16,128,2048]{2,1,0:T(8,128)(2,1)} %bitcast.104, bf16[16,128,128]{2,1,0:T(8,128)(2,1)S(1)} %copy-done), kind=kOutput, calls=%fused_computation.39 | convolution fusion | flops 1073741824 | bytes 25690112 | tf_op jit(solution)/shard_map/jbt,jbl->tjl/dot_general | solution.py:12
  251.1 26.2 %fusion.6 = bf16[2048,16,128]{2,0,1:T(8,128)(2,1)} fusion(f32[16,2048,128]{2,1,0:T(8,128)} %fusion.39, bf16[16,128,128]{2,1,0:T(8,128)(2,1)S(1)} %copy-done.5, bf16[128,16,2048]{2,1,0:T(8,128)(2,1)} %bitcast.112), kind=kOutput, calls=%fused_computation.8 | convolution fusion | flops 1157627904 | bytes 34078720 | tf_op jit(solution)/shard_map/jbt,bkj->tbk/dot_general | solution.py:12
  277.4 9.1 %convert_bitcast_fusion = bf16[16,128,2048]{1,2,0:T(8,128)(2,1)} fusion(bf16[2048,16,128]{2,0,1:T(8,128)(2,1)} %fusion.6, bf16[16,128,128]{2,1,0:T(8,128)(2,1)S(1)} %copy-done), kind=kOutput, calls=%fused_computation.24 | convolution fusion | flops 1077936128 | bytes 17301504 | tf_op jit(solution)/shard_map/tjl,jbl->jbt/dot_general | solution.py:12
  286.5 12.5 %copy.81 = bf16[16,128,2048]{2,0,1:T(8,128)(2,1)} copy(bf16[16,128,2048]{1,2,0:T(8,128)(2,1)} %convert_bitcast_fusion) | data formatting | bytes 16777216 | tf_op jit(solution)/shard_map/convert_element_type | solution.py:41
  299.0 5.0 all-to-all-start.3
  304.0 11.1 %convert_bitcast_fusion.1 = bf16[128,16,2048]{0,2,1:T(8,128)(2,1)} fusion(bf16[16,128,128]{2,1,0:T(8,128)(2,1)S(1)} %copy-done.5, f32[16,2048,128]{2,1,0:T(8,128)} %fusion.39), kind=kOutput, calls=%fused_computation.25 | convolution fusion | flops 1115684864 | bytes 25690112 | tf_op jit(solution)/shard_map/tbk,bkj->jbt/dot_general | solution.py:12
  315.1 12.6 %copy.73 = bf16[128,16,2048]{2,1,0:T(8,128)(2,1)} copy(bf16[128,16,2048]{0,2,1:T(8,128)(2,1)} %convert_bitcast_fusion.1) | data formatting | bytes 16777216 | tf_op jit(solution)/shard_map/convert_element_type | solution.py:30
  327.7 70.4 %all-to-all-done.3 = bf16[16,128,2048]{2,0,1:T(8,128)(2,1)} async-done(((bf16[16,128,2048]{2,0,1:T(8,128)(2,1)}), bf16[16,128,2048]{2,0,1:T(8,128)(2,1)}, u32[]{:S(2)}, u32[]{:S(2)}) %all-to-all-start.3) | async-done | bytes 8388640 | tf_op jit(solution)/shard_map/all_to_all | solution.py:44
  398.1 5.0 all-to-all-start.1
  403.1 8.3 %copy.83 = bf16[8,16,16,2048]{3,1,0,2:T(8,128)(2,1)} copy(bf16[8,16,16,2048]{3,1,2,0:T(8,128)(2,1)} %bitcast.19) | data formatting | bytes 16777216 | tf_op jit(solution)/shard_map/all_to_all | solution.py:44
  411.3 8.4 %fusion.34 = f32[16,128,128]{1,2,0:T(8,128)S(1)} fusion(bf16[128,16,2048]{2,0,1:T(8,128)(2,1)} %bitcast.106, bf16[2048,2048]{1,0:T(8,128)(2,1)} %param.6), kind=kOutput, calls=%fused_computation.38 | convolution fusion | flops 1073741824 | bytes 17825792 | tf_op jit(solution)/shard_map/tbk,jbt->bkj/dot_general | solution.py:12
  419.7 1.4 copy.85
  421.4 9.2 %fusion.40 = f32[16,128,128]{2,1,0:T(8,128)} fusion(bf16[16,128,2048]{2,1,0:T(8,128)(2,1)} %bitcast.105, bf16[2048,16,128]{2,0,1:T(8,128)(2,1)} %fusion.6), kind=kOutput, calls=%fused_computation.40 | convolution fusion | flops 1073741824 | bytes 17825792 | tf_op jit(solution)/shard_map/jbt,tjl->jbl/dot_general | solution.py:12
  430.7 19.4 %fusion.25 = f32[16,128,128]{2,1,0:T(8,128)} fusion(bf16[128,16,2048]{2,1,0:T(8,128)(2,1)} %bitcast.113, f32[16,2048,128]{2,1,0:T(8,128)} %fusion.39), kind=kOutput, calls=%fused_computation.33 | convolution fusion | flops 1111490560 | bytes 26214400 | tf_op jit(solution)/shard_map/tbk,jbt->bkj/dot_general | solution.py:12
  450.4 46.7 %all-to-all-done.1 = bf16[128,16,2048]{2,1,0:T(8,128)(2,1)} async-done(((bf16[128,16,2048]{2,1,0:T(8,128)(2,1)}), bf16[128,16,2048]{2,1,0:T(8,128)(2,1)}, u32[]{:S(2)}, u32[]{:S(2)}) %all-to-all-start.1) | async-done | bytes 8388640 | tf_op jit(solution)/shard_map/all_to_all | solution.py:31
  497.1 8.5 %copy.74 = bf16[16,8,16,2048]{3,2,1,0:T(8,128)(2,1)} copy(bf16[16,8,16,2048]{3,2,0,1:T(8,128)(2,1)} %bitcast.7) | data formatting | bytes 16777216 | tf_op jit(solution)/shard_map/all_to_all | solution.py:31
  505.6 9.5 %fusion.11 = f32[16,128,128]{2,1,0:T(8,128)} fusion(bf16[16,128,2048]{2,1,0:T(8,128)(2,1)} %bitcast.109, bf16[2048,2048]{1,0:T(8,128)(2,1)} %param.11), kind=kOutput, calls=%fused_computation.16 | convolution fusion | flops 1073741824 | bytes 17825792 | tf_op jit(solution)/shard_map/jbt,tjl->jbl/dot_general | solution.py:12
  515.1 8.9 %convolution_convert_fusion = bf16[16,2048,128]{1,2,0:T(8,128)(2,1)} fusion(bf16[16,128,128]{2,1,0:T(8,128)(2,1)S(1)} %copy-done.2, bf16[128,16,2048]{2,0,1:T(8,128)(2,1)} %bitcast.107), kind=kOutput, calls=%fused_computation.36 | convolution fusion | flops 1077936128 | bytes 17301504 | tf_op jit(solution)/shard_map/jbt,bkj->tbk/dot_general | solution.py:12
  524.1 12.3 %copy.90 = bf16[2048,2048]{1,0:T(8,128)(2,1)} copy(bf16[2048,2048]{0,1:T(8,128)(2,1)} %bitcast.108) | data formatting | bytes 16777216
  536.4 9.0 %convolution_convert_fusion.1 = bf16[16,2048,128]{1,2,0:T(8,128)(2,1)} fusion(bf16[16,128,2048]{2,1,0:T(8,128)(2,1)} %bitcast.110, bf16[16,128,128]{2,1,0:T(8,128)(2,1)S(1)} %copy-done.4), kind=kOutput, calls=%fused_computation.37 | convolution fusion | flops 1077936128 | bytes 17301504 | tf_op jit(solution)/shard_map/jbt,jbl->tjl/dot_general | solution.py:12
  545.4 12.3 %copy.89 = bf16[2048,2048]{1,0:T(8,128)(2,1)} copy(bf16[2048,2048]{0,1:T(8,128)(2,1)} %bitcast.111) | data formatting | bytes 16777216
  557.7 1.7 copy.91
  (24 shorter events, 0.7 us)
Async XLA Ops:
  7.2 232.3 %copy-start = (bf16[16,128,128]{2,1,0:T(8,128)(2,1)S(1)}, bf16[16,128,128]{2,1,0:T(8,128)(2,1)}, u32[]{:S(2)}) copy-start(bf16[16,128,128]{2,1,0:T(8,128)(2,1)} %param.8) | copy-start | bytes 1572868
  28.1 5.6 copy-start.3
  28.1 100.0 %all-to-all-start = ((bf16[128,16,2048]{2,1,0:T(8,128)(2,1)}), bf16[128,16,2048]{2,1,0:T(8,128)(2,1)}, u32[]{:S(2)}, u32[]{:S(2)}) async-start(bf16[128,16,2048]{2,1,0:T(8,128)(2,1)} %copy.70), calls=%async_computation | async-start | bytes 16777216 | tf_op jit(solution)/shard_map/all_to_all | solution.py:27
  128.1 99.3 %all-to-all-start.2 = ((bf16[16,128,2048]{2,0,1:T(8,128)(2,1)}), bf16[16,128,2048]{2,0,1:T(8,128)(2,1)}, u32[]{:S(2)}, u32[]{:S(2)}) async-start(bf16[16,128,2048]{2,0,1:T(8,128)(2,1)} %copy.77), calls=%async_computation.2 | async-start | bytes 16777216 | tf_op jit(solution)/shard_map/all_to_all | solution.py:17
  239.5 11.7 %copy-start.5 = (bf16[16,128,128]{2,1,0:T(8,128)(2,1)S(1)}, bf16[16,128,128]{2,1,0:T(8,128)(2,1)}, u32[]{:S(2)}) copy-start(bf16[16,128,128]{2,1,0:T(8,128)(2,1)} %param.9) | copy-start | bytes 1572868
  299.0 99.0 %all-to-all-start.3 = ((bf16[16,128,2048]{2,0,1:T(8,128)(2,1)}), bf16[16,128,2048]{2,0,1:T(8,128)(2,1)}, u32[]{:S(2)}, u32[]{:S(2)}) async-start(bf16[16,128,2048]{2,0,1:T(8,128)(2,1)} %copy.81), calls=%async_computation.3 | async-start | bytes 16777216 | tf_op jit(solution)/shard_map/all_to_all | solution.py:44
  398.1 99.0 %all-to-all-start.1 = ((bf16[128,16,2048]{2,1,0:T(8,128)(2,1)}), bf16[128,16,2048]{2,1,0:T(8,128)(2,1)}, u32[]{:S(2)}, u32[]{:S(2)}) async-start(bf16[128,16,2048]{2,1,0:T(8,128)(2,1)} %copy.73), calls=%async_computation.1 | async-start | bytes 16777216 | tf_op jit(solution)/shard_map/all_to_all | solution.py:31
  403.0 154.6 %reduce-scatter.5.cloned.1.call-start = ((), (), s32[]{:S(2)}) async-start(), calls=%async_computation.8 | async-start | bytes 1310720 | tf_op jit(solution)/shard_map/reduce_scatter | solution.py:47
  421.2 138.2 %reduce-scatter.7.cloned.1.call-start = ((), (), s32[]{:S(2)}) async-start(), calls=%async_computation.9 | async-start | bytes 1310720 | tf_op jit(solution)/shard_map/reduce_scatter | solution.py:43
  430.6 128.8 %reduce-scatter.9.cloned.1.call-start = ((), (), s32[]{:S(2)}) async-start(), calls=%async_computation.10 | async-start | bytes 1310720 | tf_op jit(solution)/shard_map/reduce_scatter | solution.py:38
  450.1 109.4 %reduce-scatter.11.cloned.1.call-start = ((), (), s32[]{:S(2)}) async-start(), calls=%async_computation.11 | async-start | bytes 1310720 | tf_op jit(solution)/shard_map/reduce_scatter | solution.py:34
  505.6 9.5 %copy-start.2 = (bf16[16,128,128]{2,1,0:T(8,128)(2,1)S(1)}, bf16[16,128,128]{2,1,0:T(8,128)(2,1)}, u32[]{:S(2)}) copy-start(bf16[16,128,128]{2,1,0:T(8,128)(2,1)} %param.7) | copy-start | bytes 1572868
  524.1 12.3 %copy-start.4 = (bf16[16,128,128]{2,1,0:T(8,128)(2,1)S(1)}, bf16[16,128,128]{2,1,0:T(8,128)(2,1)}, u32[]{:S(2)}) copy-start(bf16[16,128,128]{2,1,0:T(8,128)(2,1)} %param.10) | copy-start | bytes 1572868
  545.4 14.0 %copy-start.1 = (bf16[16,128,128]{2,1,0:T(8,128)(2,1)S(1)}, bf16[16,128,128]{2,1,0:T(8,128)(2,1)}, u32[]{:S(2)}) copy-start(bf16[16,128,128]{2,1,0:T(8,128)(2,1)} %param.8) | copy-start | bytes 1572868
Sparse Core Ops, SparseCore 0:
  421.3 29.5 reduce-scatter.4
  453.9 25.8 reduce-scatter.6
  482.6 25.7 reduce-scatter.8
  515.2 27.3 reduce-scatter.10
where the time goes:
time: 574 us; the launch traced here: 566 us
  waiting for transfers between devices  277 us (48%)
  matrix products  141 us (25%)
  local copies, waits for them, and re-layouts  113 us (20%)
  starting transfers between devices  21.3 us (4%)
  between operations  14.3 us (2%)
    dot_general x12, matrix products, product(): return jnp.einsum(form, left, right, preferred_element_type=jnp.float32)  141 us
    all_to_all x1, waiting for transfers between devices, return_second(): lax.all_to_all(grad_perm_two, 'mp', split_axis=1, concat_axis=0, tiled=True)  85.6 us
    all_to_all x1, waiting for transfers between devices, body(): lax.all_to_all(first_mid, 'mp', split_axis=0, concat_axis=1, tiled=True)  74 us
    all_to_all x1, waiting for transfers between devices, body(): lax.all_to_all(grad_perm_one, 'mp', split_axis=1, concat_axis=0, tiled=True)  70.4 us
    all_to_all x1, waiting for transfers between devices, body(): lax.all_to_all(second_mid, 'mp', split_axis=0, concat_axis=1, tiled=True)  46.7 us
    unnamed x15, local copies, waits for them, and re-layouts  26.3 us
    convert_element_type x1, local copies, waits for them, and re-layouts, body(): second_mid = product('tbk,bkj->jbt', hidden, inner_two).astype(jnp.bfloat16)  12.6 us
    convert_element_type x1, local copies, waits for them, and re-layouts, body(): product('tjl,jbl->jbt', grad_pre, outer_one).astype(jnp.bfloat16)  12.5 us
  transfers between devices with their start and end apart: 8, of which 4 were waited for; matrix products, arithmetic and copies ran while one was open for 28% of the time, Pallas kernels for 0%

commit v1 on v0

v1 whole, which is shorter than its diff:
```python
import jax
import jax.numpy as jnp
from jax import lax
from jax.sharding import PartitionSpec as P

PARTS = 2


def gelu_tanh(values):
    return jax.nn.gelu(values, approximate=True)


def product(form, left, right):
    return jnp.einsum(form, left, right, preferred_element_type=jnp.float32)


def forward(values):
    return lax.all_to_all(values, "mp", split_axis=0, concat_axis=1, tiled=True)


def back(values):
    return lax.all_to_all(values, "mp", split_axis=1, concat_axis=0, tiled=True)


def after(value, earlier):
    return lax.optimization_barrier((value, earlier))[0]


def body(tokens, inner_one, outer_one, inner_two, outer_two, cotangent):
    tok_rows = tokens.shape[0]
    local_blocks = inner_one.shape[0]
    block_size = inner_one.shape[1]
    rows = tok_rows // PARTS
    inputs, grads, first_perm, grad_mid_two = [], [], [], []
    arrived = None
    for part in range(PARTS):
        cut = slice(part * rows, (part + 1) * rows)
        x_part = tokens[cut].reshape(rows, local_blocks, block_size)
        g_part = cotangent[cut].reshape(rows, local_blocks, block_size)
        inputs.append(x_part)
        grads.append(g_part)
        first_mid = product("tbk,bkj->jbt", x_part, inner_one).astype(jnp.bfloat16)
        if arrived is None:
            g_part = after(g_part, first_mid)
        else:
            first_mid = after(first_mid, arrived)
        arrived = forward(first_mid)
        first_perm.append(arrived)
        grad_perm_two = product("tjl,jbl->jbt", g_part, outer_two).astype(jnp.bfloat16)
        arrived = back(after(grad_perm_two, arrived))
        grad_mid_two.append(arrived)
    second_perm, grad_mid_one = [], []
    inner_two_grad = outer_one_grad = outer_two_grad = inner_one_grad = 0.0
    output, input_grad = [], []
    for part in range(PARTS):
        pre_act = product("jbt,jbl->tjl", first_perm[part], outer_one)
        hidden = gelu_tanh(pre_act).astype(jnp.bfloat16)
        second_mid = product("tbk,bkj->jbt", hidden, inner_two).astype(jnp.bfloat16)
        arrived = forward(after(second_mid, arrived))
        second_perm.append(arrived)
        grad_hidden = product("jbt,bkj->tbk", grad_mid_two[part], inner_two)
        inner_two_grad += product("tbk,jbt->bkj", hidden, grad_mid_two[part])
        primal_out, pullback = jax.vjp(gelu_tanh, pre_act)
        grad_pre = pullback(grad_hidden)[0].astype(jnp.bfloat16)
        grad_perm_one = product("tjl,jbl->jbt", grad_pre, outer_one).astype(jnp.bfloat16)
        arrived = back(after(grad_perm_one, arrived))
        grad_mid_one.append(arrived)
        outer_one_grad += product("jbt,tjl->jbl", first_perm[part], grad_pre)
    for part in range(PARTS):
        output.append(product("jbt,jbl->tjl", second_perm[part], outer_two).astype(jnp.bfloat16))
        outer_two_grad += product("jbt,tjl->jbl", second_perm[part], grads[part])
        inner_one_grad += product("tbk,jbt->bkj", inputs[part], grad_mid_one[part])
        input_grad.append(product("jbt,bkj->tbk", grad_mid_one[part], inner_one).astype(jnp.bfloat16))

    def total(grad):
        return lax.psum_scatter(grad, "dp", scatter_dimension=1, tiled=True)

    width_here = local_blocks * block_size
    return (
        jnp.concatenate(output).reshape(tok_rows, width_here),
        jnp.concatenate(input_grad).reshape(tok_rows, width_here),
        total(inner_one_grad),
        total(outer_one_grad),
        total(inner_two_grad),
        total(outer_two_grad),
    )


def solution(mesh):
    placed = (
        P("dp", "mp"),
        P("mp", None, None),
        P("mp", None, None),
        P("mp", None, None),
        P("mp", None, None),
        P("dp", "mp"),
    )
    return jax.shard_map(
        body,
        mesh=mesh,
        in_specs=placed,
        out_specs=(
            P("dp", "mp"),
            P("dp", "mp"),
            P("mp", "dp", None),
            P("mp", "dp", None),
            P("mp", "dp", None),
            P("mp", "dp", None),
        ),
        check_vma=False,
    )
```

time: 574 us -> 702 us (1.22)
  local copies, waits for them, and re-layouts: 113 us -> 197 us
  blocking collectives: 0 us -> 53.1 us
  waiting for transfers between devices: 277 us -> 244 us
  other arithmetic: 0 us -> 15.4 us
  starting transfers between devices: 21.3 us -> 34.6 us
    all_to_all x0 -> x1, blocking collectives: none -> 53.1 us  [back(): return lax.all_to_all(values, 'mp', split_axis=1, concat_axis=0, tiled=True)]
    convert_element_type x4 -> x1, local copies, waits for them, and re-layouts: 47.7 us -> 4.34 us  [body(): first_mid = product('tbk,bkj->jbt', x_part, inner_one).astype(jnp.bfloat16)]
    optimization_barrier x0 -> x7, local copies, waits for them, and re-layouts: none -> 42.5 us  [after(): return lax.optimization_barrier((value, earlier))[0]]
    unnamed x15 -> x53, local copies, waits for them, and re-layouts: 26.3 us -> 68.4 us
    all_to_all x4 -> x7, waiting for transfers between devices: 277 us -> 243 us  [the longest x4 131 us: forward(): return lax.all_to_all(values, 'mp', split_axis=0, concat_axis=1, tiled=True)]
    concatenate x0 -> x2, local copies, waits for them, and re-layouts: none -> 25 us  [the longest x1 12.6 us: body(): jnp.concatenate(output).reshape(tok_rows, width_here)]
    concatenate x0 -> x2, other arithmetic: none -> 15.4 us  [the longest x1 7.73 us: body(): jnp.concatenate(output).reshape(tok_rows, width_here)]
    all_to_all x4 -> x7, starting transfers between devices: 20.7 us -> 33.9 us  [the longest x4 19.4 us: forward(): return lax.all_to_all(values, 'mp', split_axis=0, concat_axis=1, tiled=True)]
  transfers between devices with their start and end apart: 8 -> 11, of which waited for: 4 -> 7; matrix products, arithmetic and copies ran while one was open for 28% -> 31% of each run, Pallas kernels for 0% -> 0%
where the time goes in v1:
time: 702 us; the launch traced here: 692 us
  waiting for transfers between devices  244 us (35%)
  local copies, waits for them, and re-layouts  197 us (28%)
  matrix products  134 us (19%)
  blocking collectives  53.1 us (8%)
  starting transfers between devices  34.6 us (5%)
  other arithmetic  15.4 us (2%)
  between operations  14.5 us (2%)
    dot_general x24, matrix products, product(): return jnp.einsum(form, left, right, preferred_element_type=jnp.float32)  134 us
    all_to_all x4, waiting for transfers between devices, forward(): return lax.all_to_all(values, 'mp', split_axis=0, concat_axis=1, tiled=True)  131 us
    all_to_all x3, waiting for transfers between devices, back(): return lax.all_to_all(values, 'mp', split_axis=1, concat_axis=0, tiled=True)  113 us
    unnamed x53, local copies, waits for them, and re-layouts  68.4 us
    all_to_all x1, blocking collectives, back(): return lax.all_to_all(values, 'mp', split_axis=1, concat_axis=0, tiled=True)  53.1 us
    optimization_barrier x7, local copies, waits for them, and re-layouts, after(): return lax.optimization_barrier((value, earlier))[0]  42.5 us
    all_to_all x4, local copies, waits for them, and re-layouts, back(): return lax.all_to_all(values, 'mp', split_axis=1, concat_axis=0, tiled=True)  23.2 us
    all_to_all x4, local copies, waits for them, and re-layouts, forward(): return lax.all_to_all(values, 'mp', split_axis=0, concat_axis=1, tiled=True)  20.2 us
  transfers between devices with their start and end apart: 11, of which 7 were waited for; matrix products, arithmetic and copies ran while one was open for 31% of the time, Pallas kernels for 0%

profile of v1, /device:TPU:0, one launch (start us, length us, event | category | flops | bytes accessed | tf_op | source)
XLA Modules:
  0.0 692.4 jit_solution(14782064879570913023)
XLA Ops:
  13.4 6.5 copy.203
  39.0 6.5 copy.206
  51.0 31.2 %all-to-all-done = bf16[128,16,1024]{2,1,0:T(8,128)(2,1)} async-done(((bf16[128,16,1024]{2,1,0:T(8,128)(2,1)}), bf16[128,16,1024]{2,1,0:T(8,128)(2,1)}, u32[]{:S(2)}, u32[]{:S(2)}) %all-to-all-start) | async-done | bytes 4194336 | tf_op jit(solution)/shard_map/all_to_all | solution.py:18
  87.1 6.8 copy.142
  98.7 6.5 copy.205
  110.7 37.1 %all-to-all-done.1 = bf16[16,128,1024]{2,0,1:T(8,128)(2,1)} async-done(((bf16[16,128,1024]{2,0,1:T(8,128)(2,1)}), bf16[16,128,1024]{2,0,1:T(8,128)(2,1)}, u32[]{:S(2)}, u32[]{:S(2)}) %all-to-all-start.1) | async-done | bytes 4194336 | tf_op jit(solution)/shard_map/all_to_all | solution.py:22
  147.8 6.9 %copy.144 = bf16[8,16,16,1024]{3,2,1,0:T(8,128)(2,1)} copy(bf16[8,16,16,1024]{3,1,2,0:T(8,128)(2,1)} %bitcast.14) | data formatting | bytes 8388608 | tf_op jit(solution)/shard_map/all_to_all | solution.py:22
  163.7 6.4 copy.204
  175.6 37.2 %all-to-all-done.2 = bf16[128,16,1024]{2,1,0:T(8,128)(2,1)} async-done(((bf16[128,16,1024]{2,1,0:T(8,128)(2,1)}), bf16[128,16,1024]{2,1,0:T(8,128)(2,1)}, u32[]{:S(2)}, u32[]{:S(2)}) %all-to-all-start.2) | async-done | bytes 4194336 | tf_op jit(solution)/shard_map/all_to_all | solution.py:18
  238.6 37.8 %all-to-all-done.3 = bf16[16,128,1024]{2,0,1:T(8,128)(2,1)} async-done(((bf16[16,128,1024]{2,0,1:T(8,128)(2,1)}), bf16[16,128,1024]{2,0,1:T(8,128)(2,1)}, u32[]{:S(2)}, u32[]{:S(2)}) %all-to-all-start.3) | async-done | bytes 4194336 | tf_op jit(solution)/shard_map/all_to_all | solution.py:22
  276.4 6.8 copy.149
  283.2 6.8 copy.150
  295.1 12.6 %fusion.6 = bf16[1024,16,128]{2,0,1:T(8,128)(2,1)S(1)} fusion(f32[16,1024,128]{2,1,0:T(8,128)} %copy-done.20, bf16[16,128,128]{2,1,0:T(8,128)(2,1)S(1)} %copy-done, bf16[128,16,1024]{2,1,0:T(8,128)(2,1)} %bitcast.177), kind=kOutput, calls=%fused_computation.10 | convolution fusion | flops 578813952 | bytes 17301504 | tf_op jit(solution)/shard_map/jbt,bkj->tbk/dot_general | solution.py:14
  312.9 31.3 %all-to-all-done.4 = bf16[128,16,1024]{2,1,0:T(8,128)(2,1)} async-done(((bf16[128,16,1024]{2,1,0:T(8,128)(2,1)}), bf16[128,16,1024]{2,1,0:T(8,128)(2,1)}, u32[]{:S(2)}, u32[]{:S(2)}) %all-to-all-start.4) | async-done | bytes 4194336 | tf_op jit(solution)/shard_map/all_to_all | solution.py:18
  349.3 6.8 copy.155
  372.1 37.8 %all-to-all-done.5 = bf16[16,128,1024]{2,0,1:T(8,128)(2,1)} async-done(((bf16[16,128,1024]{2,0,1:T(8,128)(2,1)}), bf16[16,128,1024]{2,0,1:T(8,128)(2,1)}, u32[]{:S(2)}, u32[]{:S(2)}) %all-to-all-start.5) | async-done | bytes 4194336 | tf_op jit(solution)/shard_map/all_to_all | solution.py:22
  409.9 6.8 copy.157
  416.7 6.7 copy.158
  428.3 12.6 %fusion.13 = bf16[1024,16,128]{2,0,1:T(8,128)(2,1)S(1)} fusion(f32[16,1024,128]{2,1,0:T(8,128)} %copy-done.21, bf16[16,128,128]{2,1,0:T(8,128)(2,1)S(1)} %copy-done, bf16[128,16,1024]{2,1,0:T(8,128)(2,1)} %bitcast.179), kind=kOutput, calls=%fused_computation.17 | convolution fusion | flops 578813952 | bytes 17301504 | tf_op jit(solution)/shard_map/jbt,bkj->tbk/dot_general | solution.py:14
  446.2 31.0 %all-to-all-done.6 = bf16[128,16,1024]{2,1,0:T(8,128)(2,1)} async-done(((bf16[128,16,1024]{2,1,0:T(8,128)(2,1)}), bf16[128,16,1024]{2,1,0:T(8,128)(2,1)}, u32[]{:S(2)}, u32[]{:S(2)}) %all-to-all-start.6) | async-done | bytes 4194336 | tf_op jit(solution)/shard_map/all_to_all | solution.py:18
  482.2 6.8 copy.164
  489.0 53.1 %all_to_all.144 = bf16[16,128,1024]{2,0,1:T(8,128)(2,1)S(1)} all-to-all(bf16[16,128,1024]{2,0,1:T(8,128)(2,1)} %copy.164), channel_id=1, replica_groups=mesh['dp'=4,'mp'=8] {'mp'}, dimensions={1} | all-to-all | bytes 8388608 | tf_op jit(solution)/shard_map/all_to_all | solution.py:22
  564.7 11.3 %fusion.24 = f32[16,128,128]{2,1,0:T(8,128)S(1)} fusion(bf16[128,16,1024]{2,1,0:T(8,128)(2,1)} %bitcast.180, f32[16,1024,128]{2,1,0:T(8,128)} %copy-done.21), kind=kOutput, calls=%fused_computation.47 | convolution fusion | flops 555745280 | bytes 13631488 | tf_op jit(solution)/shard_map/tbk,jbt->bkj/dot_general | solution.py:14
  576.0 9.5 %fusion.52 = f32[16,128,128]{2,1,0:T(8,128)} fusion(f32[16,128,128]{2,1,0:T(8,128)S(1)} %fusion.24, bf16[128,16,1024]{2,1,0:T(8,128)(2,1)S(1)} %bitcast.178, f32[16,1024,128]{2,1,0:T(8,128)} %copy-done.20), kind=kOutput, calls=%fused_computation.66 | convolution fusion | flops 556007424 | bytes 14680064 | tf_op jit(solution)/shard_map/tbk,jbt->bkj/dot_general | solution.py:14
  597.5 9.0 %convert_bitcast_fusion.2 = bf16[1024,16,128]{2,0,1:T(8,128)(2,1)} fusion(bf16[16,128,128]{2,1,0:T(8,128)(2,1)S(1)} %copy-done.19, bf16[128,16,1024]{2,1,0:T(8,128)(2,1)} %bitcast.172), kind=kOutput, calls=%fused_computation.36 | convolution fusion | flops 538968064 | bytes 8912896 | tf_op jit(solution)/shard_map/jbt,bkj->tbk/dot_general | solution.py:14
  609.9 7.7 %pad_maximum_fusion = bf16[2048,16,128]{2,0,1:T(8,128)(2,1)} fusion(bf16[1024,16,128]{2,0,1:T(8,128)(2,1)} %convert_bitcast_fusion.3, bf16[1024,16,128]{2,0,1:T(8,128)(2,1)} %convert_bitcast_fusion.6), kind=kLoop, calls=%fused_computation.18 | loop fusion | flops 16777216 | bytes 16777216 | tf_op jit(solution)/shard_map/concatenate | solution.py:80
  617.6 12.6 %copy.161 = bf16[2048,16,128]{0,2,1:T(8,128)(2,1)} copy(bf16[2048,16,128]{2,0,1:T(8,128)(2,1)} %pad_maximum_fusion) | data formatting | bytes 16777216 | tf_op jit(solution)/shard_map/concatenate | solution.py:80
  630.2 12.2 %copy.180 = bf16[2048,2048]{1,0:T(8,128)(2,1)} copy(bf16[2048,2048]{0,1:T(8,128)(2,1)} %bitcast.166) | data formatting | bytes 16777216
  642.5 8.8 %convert_bitcast_fusion = bf16[1024,16,128]{2,0,1:T(8,128)(2,1)} fusion(bf16[16,128,128]{2,1,0:T(8,128)(2,1)S(1)} %copy-done.19, bf16[128,16,1024]{2,1,0:T(8,128)(2,1)} %bitcast.175), kind=kOutput, calls=%fused_computation.34 | convolution fusion | flops 538968064 | bytes 8912896 | tf_op jit(solution)/shard_map/jbt,bkj->tbk/dot_general | solution.py:14
  651.3 7.7 %pad_maximum_fusion.1 = bf16[2048,16,128]{2,0,1:T(8,128)(2,1)} fusion(bf16[1024,16,128]{2,0,1:T(8,128)(2,1)} %convert_bitcast_fusion, bf16[1024,16,128]{2,0,1:T(8,128)(2,1)} %convert_bitcast_fusion.2), kind=kLoop, calls=%fused_computation.19 | loop fusion | flops 16777216 | bytes 16777216 | tf_op jit(solution)/shard_map/concatenate | solution.py:81
  659.0 12.4 %copy.168 = bf16[2048,16,128]{0,2,1:T(8,128)(2,1)} copy(bf16[2048,16,128]{2,0,1:T(8,128)(2,1)} %pad_maximum_fusion.1) | data formatting | bytes 16777216 | tf_op jit(solution)/shard_map/concatenate | solution.py:81
  671.4 12.3 %copy.181 = bf16[2048,2048]{1,0:T(8,128)(2,1)} copy(bf16[2048,2048]{0,1:T(8,128)(2,1)} %bitcast.167) | data formatting | bytes 16777216
  (95 shorter events, 172.3 us)
Async XLA Ops:
  7.2 227.1 %copy-start = (bf16[16,128,128]{2,1,0:T(8,128)(2,1)S(1)}, bf16[16,128,128]{2,1,0:T(8,128)(2,1)}, u32[]{:S(2)}) copy-start(bf16[16,128,128]{2,1,0:T(8,128)(2,1)} %param.9) | copy-start | bytes 1572868
  13.4 6.6 copy-start.19
  27.8 54.4 %all-to-all-start = ((bf16[128,16,1024]{2,1,0:T(8,128)(2,1)}), bf16[128,16,1024]{2,1,0:T(8,128)(2,1)}, u32[]{:S(2)}, u32[]{:S(2)}) async-start(bf16[128,16,1024]{2,1,0:T(8,128)(2,1)} %copy.132), calls=%async_computation | async-start | bytes 8388608 | tf_op jit(solution)/shard_map/all_to_all | solution.py:18
  39.0 6.5 copy-start.18
  93.9 53.9 %all-to-all-start.1 = ((bf16[16,128,1024]{2,0,1:T(8,128)(2,1)}), bf16[16,128,1024]{2,0,1:T(8,128)(2,1)}, u32[]{:S(2)}, u32[]{:S(2)}) async-start(bf16[16,128,1024]{2,0,1:T(8,128)(2,1)} %copy.142), calls=%async_computation.1 | async-start | bytes 8388608 | tf_op jit(solution)/shard_map/all_to_all | solution.py:22
  147.8 6.9 %copy-start.15 = (bf16[128,16,1024]{2,0,1:T(8,128)(2,1)S(1)}, bf16[128,16,1024]{2,0,1:T(8,128)(2,1)}, u32[]{:S(2)}) copy-start(bf16[128,16,1024]{2,0,1:T(8,128)(2,1)} %convert_bitcast_fusion.8) | copy-start | bytes 12582916
  159.1 53.7 %all-to-all-start.2 = ((bf16[128,16,1024]{2,1,0:T(8,128)(2,1)}), bf16[128,16,1024]{2,1,0:T(8,128)(2,1)}, u32[]{:S(2)}, u32[]{:S(2)}) async-start(bf16[128,16,1024]{2,1,0:T(8,128)(2,1)} %copy.145), calls=%async_computation.2 | async-start | bytes 8388608 | tf_op jit(solution)/shard_map/all_to_all | solution.py:18
  212.8 5.2 copy-start.16
  222.3 5.0 copy-start.17
  222.3 54.1 %all-to-all-start.3 = ((bf16[16,128,1024]{2,0,1:T(8,128)(2,1)}), bf16[16,128,1024]{2,0,1:T(8,128)(2,1)}, u32[]{:S(2)}, u32[]{:S(2)}) async-start(bf16[16,128,1024]{2,0,1:T(8,128)(2,1)} %copy.147), calls=%async_computation.3 | async-start | bytes 8388608 | tf_op jit(solution)/shard_map/all_to_all | solution.py:22
  230.8 3.4 copy-start.20
  290.0 54.2 %all-to-all-start.4 = ((bf16[128,16,1024]{2,1,0:T(8,128)(2,1)}), bf16[128,16,1024]{2,1,0:T(8,128)(2,1)}, u32[]{:S(2)}, u32[]{:S(2)}) async-start(bf16[128,16,1024]{2,1,0:T(8,128)(2,1)} %copy.150), calls=%async_computation.4 | async-start | bytes 8388608 | tf_op jit(solution)/shard_map/all_to_all | solution.py:18
  356.0 53.9 %all-to-all-start.5 = ((bf16[16,128,1024]{2,0,1:T(8,128)(2,1)}), bf16[16,128,1024]{2,0,1:T(8,128)(2,1)}, u32[]{:S(2)}, u32[]{:S(2)}) async-start(bf16[16,128,1024]{2,0,1:T(8,128)(2,1)} %copy.155), calls=%async_computation.5 | async-start | bytes 8388608 | tf_op jit(solution)/shard_map/all_to_all | solution.py:22
  364.3 3.4 copy-start.21
  423.5 53.7 %all-to-all-start.6 = ((bf16[128,16,1024]{2,1,0:T(8,128)(2,1)}), bf16[128,16,1024]{2,1,0:T(8,128)(2,1)}, u32[]{:S(2)}, u32[]{:S(2)}) async-start(bf16[128,16,1024]{2,1,0:T(8,128)(2,1)} %copy.158), calls=%async_computation.6 | async-start | bytes 8388608 | tf_op jit(solution)/shard_map/all_to_all | solution.py:18
  428.1 255.6 %reduce-scatter.5.cloned.1.call-start = ((), (), s32[]{:S(2)}) async-start(), calls=%async_computation.12 | async-start | bytes 1310720 | tf_op jit(solution)/shard_map/reduce_scatter | solution.py:76
  542.1 2.6 copy-start.9
  544.7 2.9 copy-start.11
  544.7 3.7 copy-start.8
  544.7 5.0 copy-start.10
  556.3 129.1 %reduce-scatter.7.cloned.1.call-start = ((), (), s32[]{:S(2)}) async-start(), calls=%async_computation.13 | async-start | bytes 1310720 | tf_op jit(solution)/shard_map/reduce_scatter | solution.py:76
  556.5 4.9 copy-start.2
  556.5 5.9 copy-start.14
  564.6 120.8 %reduce-scatter.9.cloned.1.call-start = ((), (), s32[]{:S(2)}) async-start(), calls=%async_computation.14 | async-start | bytes 1310720 | tf_op jit(solution)/shard_map/reduce_scatter | solution.py:76
  564.7 11.3 %copy-start.22 = (bf16[8,16,16,1024]{3,2,1,0:T(8,128)(2,1)S(1)}, bf16[8,16,16,1024]{3,2,1,0:T(8,128)(2,1)}, u32[]{:S(2)}) copy-start(bf16[8,16,16,1024]{3,2,1,0:T(8,128)(2,1)} %copy.144) | copy-start | bytes 12582916
  585.4 99.9 %reduce-scatter.11.cloned.1.call-start = ((), (), s32[]{:S(2)}) async-start(), calls=%async_computation.15 | async-start | bytes 1310720 | tf_op jit(solution)/shard_map/reduce_scatter | solution.py:76
  585.7 5.7 copy-start.3
  585.7 5.7 copy-start.5
  591.5 2.2 copy-start.4
  591.5 3.5 copy-start.6
  597.5 9.0 %copy-start.7 = (bf16[16,8,16,1024]{3,2,1,0:T(8,128)(2,1)S(1)}, bf16[16,8,16,1024]{3,2,1,0:T(8,128)(2,1)}, u32[]{:S(2)}) copy-start(bf16[16,8,16,1024]{3,2,1,0:T(8,128)(2,1)} %copy.159) | copy-start | bytes 12582916
  671.4 14.0 %copy-start.1 = (bf16[16,128,128]{2,1,0:T(8,128)(2,1)S(1)}, bf16[16,128,128]{2,1,0:T(8,128)(2,1)}, u32[]{:S(2)}) copy-start(bf16[16,128,128]{2,1,0:T(8,128)(2,1)} %param.9) | copy-start | bytes 1572868
  (2 other events, 4.0 us)
Sparse Core Ops, SparseCore 0:
  556.4 27.2 reduce-scatter.4
  586.7 25.7 reduce-scatter.6
  615.4 25.7 reduce-scatter.8
  644.0 25.7 reduce-scatter.10

commit v2 on v0

--- a/solution.py
+++ b/solution.py
@@ -1,7 +1,247 @@
+import functools
 import jax
 import jax.numpy as jnp
 from jax import lax
+from jax.experimental import pallas as pl
+from jax.experimental.pallas import tpu as pltpu
 from jax.sharding import PartitionSpec as P
+
+MESH = pl.DeviceIdType.MESH
+CHUNK = 256
+LANES = 128
+SLOTS = 2
+LAG_MIDDLE = 2
+LAG_LAST = 4
+ROOT_2_PI = 0.7978845608028654
+CUBIC = 0.044715
+
+
+def dot(left, right, left_axis, right_axis):
+    return lax.dot_general(
+        left, right, (((left_axis,), (right_axis,)), ((), ())),
+        preferred_element_type=jnp.float32,
+    )
+
+
+def monarch_kernel(
+    peers, chunks, blocks, size,
+    x_hbm, g_hbm, w1t, o1, o1t, w2, w2t, o2,
+    out_hbm, ig_hbm, i1_grad, o1_grad, i2_grad, o2_grad,
+    recv, send, stage, tiles_in, tiles_out,
+    send_sem, recv_sem, own_sem, in_sem, out_sem,
+):
+    dp, me = lax.axis_index("dp"), lax.axis_index("mp")
+    halves = CHUNK // LANES
+    copies, stores = {}, {}
+
+    barrier = pltpu.get_barrier_semaphore()
+    for step in range(1, peers):
+        pl.semaphore_signal(
+            barrier, inc=1, device_id=(dp, lax.rem(me + step, peers)), device_id_type=MESH
+        )
+
+    def load(which, source, chunk):
+        copy = pltpu.make_async_copy(
+            source.at[pl.ds(chunk * CHUNK, CHUNK)], tiles_in.at[which], in_sem.at[which]
+        )
+        copy.start()
+        copies["in", which] = copy
+
+    def store(which, target, chunk):
+        copy = pltpu.make_async_copy(
+            tiles_out.at[which], target.at[pl.ds(chunk * CHUNK, CHUNK)], out_sem.at[which]
+        )
+        copy.start()
+        stores[which] = copy
+
+    def columns(block):
+        return pl.ds(pl.multiple_of(block * size, size), size)
+
+    def spread(which, block, values):
+        for half in range(halves):
+            stage[which, half, pl.ds(block, size, stride=blocks), :] = values[
+                :, half * LANES : (half + 1) * LANES
+            ]
+
+    def release(kind, chunk):
+        for copy in copies.pop(("send", kind, chunk), ()):
+            copy.wait_send()
+
+    def dispatch(kind, chunk, which):
+        release(kind, chunk - SLOTS)
+        held = send.at[kind, chunk % SLOTS]
+        if chunk >= SLOTS:
+            copies.pop(("own", kind, chunk - SLOTS)).wait()
+
+        @pl.loop(0, size, unroll=8)
+        def _(row):
+            for half in range(halves):
+                held[row, :, half * LANES : (half + 1) * LANES] = stage[
+                    which, half, pl.ds(pl.multiple_of(row * blocks, blocks), blocks), :
+                ].astype(jnp.bfloat16)
+
+        def rows(peer):
+            return pl.ds(pl.multiple_of(peer * blocks, blocks), blocks)
+
+        place = recv.at[kind, chunk, :, rows(me), :]
+        started = []
+        for step in range(1, peers):
+            peer = lax.rem(me + step, peers)
+            copy = pltpu.make_async_remote_copy(
+                src_ref=held.at[rows(peer)],
+                dst_ref=place,
+                send_sem=send_sem.at[kind, chunk % SLOTS, step],
+                recv_sem=recv_sem.at[kind, chunk, step],
+                device_id=(dp, peer),
+                device_id_type=MESH,
+            )
+            copy.start()
+            started.append(copy)
+        copies["send", kind, chunk] = started
+        copies["recv", kind, chunk] = started
+        own = pltpu.make_async_copy(held.at[rows(me)], place, own_sem.at[kind, chunk % SLOTS])
+        own.start()
+        copies["own", kind, chunk] = own
+
+    def arrive(kind, chunk):
+        for copy in copies.pop(("recv", kind, chunk)):
+            copy.wait_recv()
+        own = copies.pop(("own", kind, chunk), None)
+        if own is not None:
+            own.wait()
+            copies["own", kind, chunk] = DONE
+
+    def first(chunk):
+        for kind, weight, source in ((0, w1t, x_hbm), (1, o2, g_hbm)):
+            copies["in", kind].wait()
+
+            @pl.loop(0, blocks, unroll=4)
+            def _(block):
+                spread(kind, block, dot(weight[block], tiles_in[kind, :, columns(block)], 1, 1))
+
+            if chunk + 1 < chunks:
+                load(kind, source, chunk + 1)
+            if kind == 0 and chunk == 0:
+                pl.semaphore_wait(barrier, peers - 1)
+            dispatch(kind, chunk, kind)
+
+    def middle(chunk):
+        arrive(0, chunk)
+        arrive(1, chunk)
+
+        @pl.loop(0, blocks, unroll=2)
+        def _(block):
+            perm = recv[0, chunk, block]
+            value = dot(o1t[block], perm, 1, 0)
+            square = value * value
+            bent = jnp.tanh(ROOT_2_PI * value * (1.0 + CUBIC * square))
+            rise = 0.5 + 0.5 * bent
+            slope = rise + (0.5 * ROOT_2_PI) * value * (1.0 - bent * bent) * (
+                1.0 + (3.0 * CUBIC) * square
+            )
+            hidden = (value * rise).astype(jnp.bfloat16)
+            back = recv[1, chunk, block]
+            grad_pre = (dot(w2[block], back, 1, 0) * slope).astype(jnp.bfloat16)
+            spread(0, block, dot(w2t[block], hidden, 1, 0))
+            spread(1, block, dot(o1[block], grad_pre, 1, 0))
+            i2_grad[block] += dot(hidden, back, 1, 1)
+            o1_grad[block] += dot(perm, grad_pre, 1, 1)
+
+        dispatch(2, chunk, 0)
+        dispatch(3, chunk, 1)
+
+    def last(chunk):
+        for kind, weight, total, source, target in (
+            (2, o2, o2_grad, g_hbm, out_hbm), (3, w1t, i1_grad, x_hbm, ig_hbm)
+        ):
+            arrive(kind, chunk)
+            copies["in", kind].wait()
+            if chunk:
+                stores[kind - 2].wait()
+
+            @pl.loop(0, blocks, unroll=4)
+            def _(block):
+                part = recv[kind, chunk, block]
+                tiles_out[kind - 2, :, columns(block)] = dot(
+                    part, weight[block], 0, 0
+                ).astype(jnp.bfloat16)
+                total[block] += dot(part, tiles_in[kind, :, columns(block)], 1, 0)
+
+            store(kind - 2, target, chunk)
+            if chunk + 1 < chunks:
+                load(kind, source, chunk + 1)
+
+    for which, source in enumerate((x_hbm, g_hbm, g_hbm, x_hbm)):
+        load(which, source, 0)
+    for total in (i1_grad, o1_grad, i2_grad, o2_grad):
+        total[...] = jnp.zeros_like(total)
+    for step in range(chunks + LAG_LAST):
+        if step < chunks:
+            first(step)
+        if 0 <= step - LAG_MIDDLE < chunks:
+            middle(step - LAG_MIDDLE)
+        if 0 <= step - LAG_LAST < chunks:
+            last(step - LAG_LAST)
+    for kind in range(4):
+        for chunk in range(chunks):
+            release(kind, chunk)
+    for copy in stores.values():
+        copy.wait()
+
+    @pl.loop(0, blocks)
+    def _(block):
+        i1_grad[block] = i1_grad[block].T
+
+
+class Done:
+    def wait(self):
+        pass
+
+
+DONE = Done()
+
+
+def fused(peers, tokens, inner_one, outer_one, inner_two, outer_two, cotangent):
+    tok_rows, width = tokens.shape
+    blocks, size, _ = inner_one.shape
+    chunks = tok_rows // CHUNK
+    in_vmem = pl.BlockSpec(memory_space=pltpu.VMEM)
+    anywhere = pl.BlockSpec(memory_space=pl.ANY)
+    grad = jax.ShapeDtypeStruct((blocks, size, size), jnp.float32)
+    wide = jax.ShapeDtypeStruct((tok_rows, width), jnp.bfloat16)
+    turned = lambda weight: jnp.swapaxes(weight, 1, 2)
+    results = pl.pallas_call(
+        functools.partial(monarch_kernel, peers, chunks, blocks, size),
+        out_shape=(wide, wide, grad, grad, grad, grad),
+        in_specs=[anywhere] * 2 + [in_vmem] * 6,
+        out_specs=(anywhere,) * 2 + (in_vmem,) * 4,
+        scratch_shapes=[
+            pltpu.VMEM((4, chunks, blocks, size, CHUNK), jnp.bfloat16),
+            pltpu.VMEM((4, SLOTS, size, blocks, CHUNK), jnp.bfloat16),
+            pltpu.VMEM((2, CHUNK // LANES, size * blocks, LANES), jnp.float32),
+            pltpu.VMEM((4, CHUNK, width), jnp.bfloat16),
+            pltpu.VMEM((2, CHUNK, width), jnp.bfloat16),
+            pltpu.SemaphoreType.DMA((4, SLOTS, peers)),
+            pltpu.SemaphoreType.DMA((4, chunks, peers)),
+            pltpu.SemaphoreType.DMA((4, SLOTS)),
+            pltpu.SemaphoreType.DMA((4,)),
+            pltpu.SemaphoreType.DMA((2,)),
+        ],
+        compiler_params=pltpu.CompilerParams(
+            collective_id=0, has_side_effects=True, vmem_limit_bytes=62 * 1024 * 1024
+        ),
+        cost_estimate=pl.CostEstimate(
+            flops=24 * tok_rows * width * size, bytes_accessed=12 * tok_rows * width,
+            transcendentals=tok_rows * width,
+        ),
+    )(
+        tokens, cotangent, turned(inner_one), outer_one, turned(outer_one),
+        inner_two, turned(inner_two), outer_two,
+    )
+    sums = [
+        lax.psum_scatter(total, "dp", scatter_dimension=1, tiled=True) for total in results[2:]
+    ]
+    return (*results[:2], *sums)
 
 
 def gelu_tanh(values):
@@ -21,6 +261,10 @@
     tok_rows = tokens.shape[0]
     local_blocks = inner_one.shape[0]
     block_size = inner_one.shape[1]
+    if local_blocks == 16 and block_size == LANES and tok_rows % CHUNK == 0:
+        return fused(
+            lax.axis_size("mp"), tokens, inner_one, outer_one, inner_two, outer_two, cotangent
+        )
     inputs = tokens.reshape(tok_rows, local_blocks, block_size)
     grads = cotangent.reshape(tok_rows, local_blocks, block_size)
     first_mid = product("tbk,bkj->jbt", inputs, inner_one).astype(jnp.bfloat16)

time: 574 us -> 528 us (0.920); the launches traced: 566 us -> 528 us
  Pallas kernels: 0 us -> 376 us
  waiting for transfers between devices: 277 us -> 115 us
  matrix products: 141 us -> 0 us
  local copies, waits for them, and re-layouts: 113 us -> 23 us
  starting transfers between devices: 21.3 us -> 0.16 us
    pallas_call x0 -> x1, Pallas kernels: none -> 376 us  [fused(): pl.pallas_call(functools.partial(monarch_kernel, peers, chunks, blocks, s...]
    all_to_all x4 -> x0, waiting for transfers between devices: 277 us -> none  [the longest x1 85.6 us: return_second(): lax.all_to_all(grad_perm_two, 'mp', split_axis=1, concat_axis=0, tiled=True)]
    dot_general x12 -> x0, matrix products: 141 us -> none  [product(): return jnp.einsum(form, left, right, preferred_element_type=jnp.float32)]
    reduce_scatter x4, waiting for transfers between devices: 0.01 us -> 113 us  [fused(): lax.psum_scatter(total, 'dp', scatter_dimension=1, tiled=True)]
    convert_element_type x4 -> x0, local copies, waits for them, and re-layouts: 47.7 us -> none  [the longest x1 12.6 us: body(): second_mid = product('tbk,bkj->jbt', hidden, inner_two).astype(jnp.bfloat16)]
    all_to_all x4 -> x0, local copies, waits for them, and re-layouts: 37.3 us -> none  [the longest x1 12.1 us: return_second(): lax.all_to_all(grad_perm_two, 'mp', split_axis=1, concat_axis=0, tiled=True)]
    all_to_all x4 -> x0, starting transfers between devices: 20.7 us -> none  [the longest x1 5.57 us: body(): lax.all_to_all(first_mid, 'mp', split_axis=0, concat_axis=1, tiled=True)]
    unnamed x15 -> x5, local copies, waits for them, and re-layouts: 26.3 us -> 23 us
  transfers between devices with their start and end apart: 8 -> 4, of which waited for: 4 -> 4; matrix products, arithmetic and copies ran while one was open for 28% -> 0% of each run, Pallas kernels for 0% -> 0%
where the time goes in v2:
time: 528 us
  Pallas kernels  376 us (71%)
  waiting for transfers between devices  115 us (22%)
  local copies, waits for them, and re-layouts  23 us (4%)
  between operations  13.8 us (3%)
    pallas_call x1, Pallas kernels, fused(): pl.pallas_call(functools.partial(monarch_kernel, peers, chunks, blocks, s...  376 us
    reduce_scatter x4, waiting for transfers between devices, fused(): lax.psum_scatter(total, 'dp', scatter_dimension=1, tiled=True)  113 us
    unnamed x5, local copies, waits for them, and re-layouts  23 us
  transfers between devices with their start and end apart: 4, of which 4 were waited for; matrix products, arithmetic and copies ran while one was open for 0% of the time, Pallas kernels for 0%

profile of v2, /device:TPU:0, one launch (start us, length us, event | category | flops | bytes accessed | tf_op | source)
XLA Modules:
  0.0 528.0 jit_solution(17059765004585997945)
XLA Ops:
  7.2 0.0 reduce-scatter.5.cloned.1.call-start
  7.2 2.0 copy.12
  9.3 2.0 copy.13
  11.3 2.0 copy.14
  13.3 376.0 %shard_map.109 = (bf16[2048,2048]{1,0:T(8,128)(2,1)}, bf16[2048,2048]{1,0:T(8,128)(2,1)}, f32[16,128,128]{2,1,0:T(8,128)}, f32[16,128,128]{2,1,0:T(8,128)}, f32[...) custom-call(bf16[2048,2048]{1,0:T(8,128)(2,1)} %x_hbm.1, bf16[2048,2048]{1,0:T(8,128)(2,1)} %g_hbm.1, ...), custom_call_target="tpu_custom_call" | custom-call | flops 12884901888 | bytes 50331648 | tf_op jit(solution)/shard_map/pallas_call | solution.py:213
  389.4 0.0 reduce-scatter.5.cloned.1.call-update
  389.4 0.0 reduce-scatter.7.cloned.1.call-start
  389.4 0.7 reduce-scatter.7.cloned.1.call-update
  390.1 0.0 reduce-scatter.9.cloned.1.call-start
  390.2 0.7 reduce-scatter.9.cloned.1.call-update
  390.9 0.0 reduce-scatter.11.cloned.1.call-start
  390.9 0.5 reduce-scatter.11.cloned.1.call-update
  391.5 27.0 %reduce-scatter.5.cloned.1.call-done = f32[16,32,128]{2,1,0:T(8,128)} async-done(((f32[16,128,128]{2,1,0:T(8,128)}), f32[16,32,128]{2,1,0:T(8,128)}) %reduce-scatter.5.cloned.1.call-update) | async-done | bytes 262160 | tf_op jit(solution)/shard_map/reduce_scatter | solution.py:242
  418.5 28.8 %reduce-scatter.7.cloned.1.call-done = f32[16,32,128]{2,1,0:T(8,128)} async-done(((f32[16,128,128]{2,1,0:T(8,128)}), f32[16,32,128]{2,1,0:T(8,128)}) %reduce-scatter.7.cloned.1.call-update) | async-done | bytes 262160 | tf_op jit(solution)/shard_map/reduce_scatter | solution.py:242
  447.2 28.7 %reduce-scatter.9.cloned.1.call-done = f32[16,32,128]{2,1,0:T(8,128)} async-done(((f32[16,128,128]{2,1,0:T(8,128)}), f32[16,32,128]{2,1,0:T(8,128)}) %reduce-scatter.9.cloned.1.call-update) | async-done | bytes 262160 | tf_op jit(solution)/shard_map/reduce_scatter | solution.py:242
  475.9 28.7 %reduce-scatter.11.cloned.1.call-done = f32[16,32,128]{2,1,0:T(8,128)} async-done(((f32[16,128,128]{2,1,0:T(8,128)}), f32[16,32,128]{2,1,0:T(8,128)}) %reduce-scatter.11.cloned.1.call-update) | async-done | bytes 262160 | tf_op jit(solution)/shard_map/reduce_scatter | solution.py:242
  504.6 8.4 %copy.17 = bf16[2048,2048]{1,0:T(8,128)(2,1)} copy(bf16[2048,2048]{1,0:T(8,128)(2,1)} %get-tuple-element.24) | data formatting | bytes 16777216
  513.0 8.4 %copy.18 = bf16[2048,2048]{1,0:T(8,128)(2,1)} copy(bf16[2048,2048]{1,0:T(8,128)(2,1)} %get-tuple-element.25) | data formatting | bytes 16777216
Async XLA Ops:
  7.2 411.3 %reduce-scatter.5.cloned.1.call-start = ((), (), s32[]{:S(2)}) async-start(), calls=%async_computation.4 | async-start | bytes 1310720 | tf_op jit(solution)/shard_map/reduce_scatter | solution.py:242
  389.4 57.9 %reduce-scatter.7.cloned.1.call-start = ((), (), s32[]{:S(2)}) async-start(), calls=%async_computation.5 | async-start | bytes 1310720 | tf_op jit(solution)/shard_map/reduce_scatter | solution.py:242
  390.1 85.8 %reduce-scatter.9.cloned.1.call-start = ((), (), s32[]{:S(2)}) async-start(), calls=%async_computation.6 | async-start | bytes 1310720 | tf_op jit(solution)/shard_map/reduce_scatter | solution.py:242
  390.9 113.7 %reduce-scatter.11.cloned.1.call-start = ((), (), s32[]{:S(2)}) async-start(), calls=%async_computation.7 | async-start | bytes 1310720 | tf_op jit(solution)/shard_map/reduce_scatter | solution.py:242
Sparse Core Ops, SparseCore 0:
  389.5 28.8 reduce-scatter.4
  421.4 25.7 reduce-scatter.6
  450.1 25.7 reduce-scatter.8
  478.7 25.8 reduce-scatter.10

commit v3 on v2

--- a/solution.py
+++ b/solution.py
@@ -12,6 +12,7 @@
 SLOTS = 2
 LAG_MIDDLE = 2
 LAG_LAST = 4
+SPARE = 16
 ROOT_2_PI = 0.7978845608028654
 CUBIC = 0.044715
 
@@ -24,20 +25,27 @@
 
 
 def monarch_kernel(
-    peers, chunks, blocks, size,
-    x_hbm, g_hbm, w1t, o1, o1t, w2, w2t, o2,
-    out_hbm, ig_hbm, i1_grad, o1_grad, i2_grad, o2_grad,
+    peers, replicas, chunks, blocks, size,
+    x_hbm, g_hbm, w1, o1, w2, o2,
+    out_hbm, ig_hbm, i1_grad, o1_sum, i2_sum, o2_sum,
     recv, send, stage, tiles_in, tiles_out,
-    send_sem, recv_sem, own_sem, in_sem, out_sem,
+    w1t, o1t, w2t, o1_grad, i2_grad, o2_grad, shares, landing,
+    send_sem, recv_sem, own_sem, in_sem, out_sem, share_sem, landing_sem,
 ):
     dp, me = lax.axis_index("dp"), lax.axis_index("mp")
     halves = CHUNK // LANES
+    slab = size // replicas
     copies, stores = {}, {}
 
     barrier = pltpu.get_barrier_semaphore()
     for step in range(1, peers):
         pl.semaphore_signal(
             barrier, inc=1, device_id=(dp, lax.rem(me + step, peers)), device_id_type=MESH
+        )
+
+    for step in range(1, replicas):
+        pl.semaphore_signal(
+            barrier, inc=1, device_id=(lax.rem(dp + step, replicas), me), device_id_type=MESH
         )
 
     def load(which, source, chunk):
@@ -111,6 +119,45 @@
             own.wait()
             copies["own", kind, chunk] = DONE
 
+    def share(which, total):
+        @pl.loop(0, blocks, unroll=4)
+        def _(block):
+            for part in range(replicas):
+                shares[which, part, block] = total[
+                    block, part * slab : (part + 1) * slab, :
+                ].astype(jnp.bfloat16)
+
+        started = []
+        for step in range(1, replicas):
+            peer = lax.rem(dp + step, replicas)
+            copy = pltpu.make_async_remote_copy(
+                src_ref=shares.at[which, peer],
+                dst_ref=landing.at[which, step],
+                send_sem=share_sem.at[which, step],
+                recv_sem=landing_sem.at[which, step],
+                device_id=(peer, me),
+                device_id_type=MESH,
+            )
+            copy.start()
+            started.append(copy)
+        copies["share", which] = started
+
+    def collect(which, total, target):
+        for copy in copies.pop(("share", which)):
+            copy.wait()
+
+        @pl.loop(0, blocks, unroll=4)
+        def _(block):
+            value = total[block, pl.ds(pl.multiple_of(dp * slab, slab), slab), :]
+            for step in range(1, replicas):
+                value += landing[which, step, block].astype(jnp.float32)
+            target[block] = value
+
+    def turn(weight, turned):
+        @pl.loop(0, blocks, unroll=4)
+        def _(block):
+            turned[block] = weight[block].T
+
     def first(chunk):
         for kind, weight, source in ((0, w1t, x_hbm), (1, o2, g_hbm)):
             copies["in", kind].wait()
@@ -122,7 +169,7 @@
             if chunk + 1 < chunks:
                 load(kind, source, chunk + 1)
             if kind == 0 and chunk == 0:
-                pl.semaphore_wait(barrier, peers - 1)
+                pl.semaphore_wait(barrier, peers + replicas - 2)
             dispatch(kind, chunk, kind)
 
     def middle(chunk):
@@ -149,6 +196,9 @@
 
         dispatch(2, chunk, 0)
         dispatch(3, chunk, 1)
+        if chunk == chunks - 1:
+            share(0, i2_grad)
+            share(1, o1_grad)
 
     def last(chunk):
         for kind, weight, total, source, target in (
@@ -170,27 +220,40 @@
             store(kind - 2, target, chunk)
             if chunk + 1 < chunks:
                 load(kind, source, chunk + 1)
+            elif kind == 2:
+                share(2, o2_grad)
 
     for which, source in enumerate((x_hbm, g_hbm, g_hbm, x_hbm)):
         load(which, source, 0)
-    for total in (i1_grad, o1_grad, i2_grad, o2_grad):
-        total[...] = jnp.zeros_like(total)
+    turn(w1, w1t)
     for step in range(chunks + LAG_LAST):
         if step < chunks:
             first(step)
+        if step == 0:
+            turn(o1, o1t)
+            turn(w2, w2t)
+            for total in (i1_grad, o1_grad, i2_grad, o2_grad):
+                @pl.loop(0, blocks, unroll=4)
+                def _(block):
+                    total[block] = jnp.zeros((size, size), jnp.float32)
         if 0 <= step - LAG_MIDDLE < chunks:
             middle(step - LAG_MIDDLE)
         if 0 <= step - LAG_LAST < chunks:
             last(step - LAG_LAST)
+
+    @pl.loop(0, blocks, unroll=4)
+    def _(block):
+        i1_grad[block] = i1_grad[block].T
+
     for kind in range(4):
         for chunk in range(chunks):
             release(kind, chunk)
     for copy in stores.values():
         copy.wait()
 
-    @pl.loop(0, blocks)
-    def _(block):
-        i1_grad[block] = i1_grad[block].T
+    collect(0, i2_grad, i2_sum)
+    collect(1, o1_grad, o1_sum)
+    collect(2, o2_grad, o2_sum)
 
 
 class Done:
@@ -201,19 +264,20 @@
 DONE = Done()
 
 
-def fused(peers, tokens, inner_one, outer_one, inner_two, outer_two, cotangent):
+def fused(peers, replicas, tokens, inner_one, outer_one, inner_two, outer_two, cotangent):
     tok_rows, width = tokens.shape
     blocks, size, _ = inner_one.shape
     chunks = tok_rows // CHUNK
     in_vmem = pl.BlockSpec(memory_space=pltpu.VMEM)
     anywhere = pl.BlockSpec(memory_space=pl.ANY)
+    slab = size // replicas
     grad = jax.ShapeDtypeStruct((blocks, size, size), jnp.float32)
-    wide = jax.ShapeDtypeStruct((tok_rows, width), jnp.bfloat16)
-    turned = lambda weight: jnp.swapaxes(weight, 1, 2)
+    part = jax.ShapeDtypeStruct((blocks, slab, size), jnp.float32)
+    wide = jax.ShapeDtypeStruct((tok_rows + SPARE, width), jnp.bfloat16)
     results = pl.pallas_call(
-        functools.partial(monarch_kernel, peers, chunks, blocks, size),
-        out_shape=(wide, wide, grad, grad, grad, grad),
-        in_specs=[anywhere] * 2 + [in_vmem] * 6,
+        functools.partial(monarch_kernel, peers, replicas, chunks, blocks, size),
+        out_shape=(wide, wide, grad, part, part, part),
+        in_specs=[anywhere] * 2 + [in_vmem] * 4,
         out_specs=(anywhere,) * 2 + (in_vmem,) * 4,
         scratch_shapes=[
             pltpu.VMEM((4, chunks, blocks, size, CHUNK), jnp.bfloat16),
@@ -221,11 +285,17 @@
             pltpu.VMEM((2, CHUNK // LANES, size * blocks, LANES), jnp.float32),
             pltpu.VMEM((4, CHUNK, width), jnp.bfloat16),
             pltpu.VMEM((2, CHUNK, width), jnp.bfloat16),
+            *[pltpu.VMEM((blocks, size, size), jnp.bfloat16)] * 3,
+            *[pltpu.VMEM((blocks, size, size), jnp.float32)] * 3,
+            pltpu.VMEM((3, replicas, blocks, slab, size), jnp.bfloat16),
+            pltpu.VMEM((3, replicas, blocks, slab, size), jnp.bfloat16),
             pltpu.SemaphoreType.DMA((4, SLOTS, peers)),
             pltpu.SemaphoreType.DMA((4, chunks, peers)),
             pltpu.SemaphoreType.DMA((4, SLOTS)),
             pltpu.SemaphoreType.DMA((4,)),
             pltpu.SemaphoreType.DMA((2,)),
+            pltpu.SemaphoreType.DMA((3, replicas)),
+            pltpu.SemaphoreType.DMA((3, replicas)),
         ],
         compiler_params=pltpu.CompilerParams(
             collective_id=0, has_side_effects=True, vmem_limit_bytes=62 * 1024 * 1024
@@ -234,14 +304,10 @@
             flops=24 * tok_rows * width * size, bytes_accessed=12 * tok_rows * width,
             transcendentals=tok_rows * width,
         ),
-    )(
-        tokens, cotangent, turned(inner_one), outer_one, turned(outer_one),
-        inner_two, turned(inner_two), outer_two,
-    )
-    sums = [
-        lax.psum_scatter(total, "dp", scatter_dimension=1, tiled=True) for total in results[2:]
-    ]
-    return (*results[:2], *sums)
+    )(tokens, cotangent, inner_one, outer_one, inner_two, outer_two)
+    output, input_grad, inner_one_term, *sums = results
+    inner_one_grad = lax.psum_scatter(inner_one_term, "dp", scatter_dimension=1, tiled=True)
+    return (output[:tok_rows], input_grad[:tok_rows], inner_one_grad, *sums)
 
 
 def gelu_tanh(values):
@@ -263,7 +329,8 @@
     block_size = inner_one.shape[1]
     if local_blocks == 16 and block_size == LANES and tok_rows % CHUNK == 0:
         return fused(
-            lax.axis_size("mp"), tokens, inner_one, outer_one, inner_two, outer_two, cotangent
+            lax.axis_size("mp"), lax.axis_size("dp"), tokens, inner_one, outer_one,
+            inner_two, outer_two, cotangent,
         )
     inputs = tokens.reshape(tok_rows, local_blocks, block_size)
     grads = cotangent.reshape(tok_rows, local_blocks, block_size)

time: 528 us -> 419 us (0.79)
  waiting for transfers between devices: 115 us -> 11.2 us
    reduce_scatter x4 -> x1, waiting for transfers between devices: 113 us -> 11.1 us  [fused(): lax.psum_scatter(inner_one_term, 'dp', scatter_dimension=1, tiled=True)]
    unnamed x5 -> x9, local copies, waits for them, and re-layouts: 23 us -> 2.12 us
    slice x0 -> x2, local copies, waits for them, and re-layouts: none -> 17 us  [fused(): return (output[:tok_rows], input_grad[:tok_rows], inner_one_grad, *sums)]
  transfers between devices with their start and end apart: 4 -> 1, of which waited for: 4 -> 1; matrix products, arithmetic and copies ran while one was open for 0% -> 4% of each run, Pallas kernels for 0% -> 0%
where the time goes in v3:
time: 419 us
  Pallas kernels  375 us (89%)
  local copies, waits for them, and re-layouts  19.1 us (5%)
  between operations  14 us (3%)
  waiting for transfers between devices  11.2 us (3%)
    pallas_call x1, Pallas kernels, fused(): pl.pallas_call(functools.partial(monarch_kernel, peers, replicas, chunks,...  375 us
    slice x2, local copies, waits for them, and re-layouts, fused(): return (output[:tok_rows], input_grad[:tok_rows], inner_one_grad, *sums)  17 us
    reduce_scatter x1, waiting for transfers between devices, fused(): lax.psum_scatter(inner_one_term, 'dp', scatter_dimension=1, tiled=True)  11.1 us
  transfers between devices with their start and end apart: 1, of which 1 were waited for; matrix products, arithmetic and copies ran while one was open for 4% of the time, Pallas kernels for 0%

profile of v3, /device:TPU:0, one launch (start us, length us, event | category | flops | bytes accessed | tf_op | source)
XLA Modules:
  0.0 419.1 jit_solution(8292913854125189024)
XLA Ops:
  7.2 0.0 reduce-scatter.2.cloned.1.call-start
  7.2 374.8 %shard_map.109 = (bf16[2064,2048]{1,0:T(8,128)(2,1)}, bf16[2064,2048]{1,0:T(8,128)(2,1)}, f32[16,128,128]{2,1,0:T(8,128)}, f32[16,32,128]{2,1,0:T(8,128)}, f32[1...) custom-call(bf16[2048,2048]{1,0:T(8,128)(2,1)} %x_hbm.1, bf16[2048,2048]{1,0:T(8,128)(2,1)} %g_hbm.1, bf16[16,128,128]{2,1,0:T(8,128)(2,1)} %w1.1, ...), custom_call_target="tpu_custom_call" | custom-call | flops 12884901888 | bytes 50331648 | tf_op jit(solution)/shard_map/pallas_call | solution.py:277
  382.0 0.0 reduce-scatter.2.cloned.1.call-update
  382.1 8.4 %slice.6 = bf16[2048,2048]{1,0:T(8,128)(2,1)} slice(bf16[2064,2048]{1,0:T(8,128)(2,1)} %get-tuple-element.12), slice={[0:2048], [0:2048]} | slice | bytes 16777216 | tf_op jit(solution)/shard_map/slice | solution.py:310
  390.5 0.0 copy-start.2
  390.5 0.0 copy-start.1
  390.5 0.0 copy-start
  390.5 8.5 %slice.7 = bf16[2048,2048]{1,0:T(8,128)(2,1)} slice(bf16[2064,2048]{1,0:T(8,128)(2,1)} %get-tuple-element.13), slice={[0:2048], [0:2048]} | slice | bytes 16777216 | tf_op jit(solution)/shard_map/slice | solution.py:310
  399.0 11.1 %reduce-scatter.2.cloned.1.call-done = f32[16,32,128]{2,1,0:T(8,128)} async-done(((f32[16,128,128]{2,1,0:T(8,128)}), f32[16,32,128]{2,1,0:T(8,128)}) %reduce-scatter.2.cloned.1.call-update) | async-done | bytes 262160 | tf_op jit(solution)/shard_map/reduce_scatter | solution.py:309
  410.2 0.0 copy-done.2
  410.2 0.7 copy.15
  410.9 0.0 copy-done.1
  410.9 0.7 copy.16
  411.6 0.0 copy-done
  411.6 0.7 copy.17
Async XLA Ops:
  7.2 403.0 %reduce-scatter.2.cloned.1.call-start = ((), (), s32[]{:S(2)}) async-start(), calls=%async_computation.1 | async-start | bytes 1310720 | tf_op jit(solution)/shard_map/reduce_scatter | solution.py:309
  390.5 19.7 %copy-start.2 = (f32[16,32,128]{2,1,0:T(8,128)S(1)}, f32[16,32,128]{2,1,0:T(8,128)}, u32[]{:S(2)}) copy-start(f32[16,32,128]{2,1,0:T(8,128)} %get-tuple-element.27) | copy-start | bytes 786436
  390.5 20.4 %copy-start.1 = (f32[16,32,128]{2,1,0:T(8,128)S(1)}, f32[16,32,128]{2,1,0:T(8,128)}, u32[]{:S(2)}) copy-start(f32[16,32,128]{2,1,0:T(8,128)} %get-tuple-element.28) | copy-start | bytes 786436
  390.5 21.1 %copy-start = (f32[16,32,128]{2,1,0:T(8,128)S(1)}, f32[16,32,128]{2,1,0:T(8,128)}, u32[]{:S(2)}) copy-start(f32[16,32,128]{2,1,0:T(8,128)} %get-tuple-element.29) | copy-start | bytes 786436
Sparse Core Ops, SparseCore 0:
  382.2 27.9 reduce-scatter.1

commit v4 on v3

--- a/solution.py
+++ b/solution.py
@@ -27,9 +27,9 @@
 def monarch_kernel(
     peers, replicas, chunks, blocks, size,
     x_hbm, g_hbm, w1, o1, w2, o2,
-    out_hbm, ig_hbm, i1_grad, o1_sum, i2_sum, o2_sum,
+    out_hbm, ig_hbm, i1_term, o1_sum, i2_sum, o2_sum,
     recv, send, stage, tiles_in, tiles_out,
-    w1t, o1t, w2t, o1_grad, i2_grad, o2_grad, shares, landing,
+    w1t, o1t, w2t, i1_grad, o1_grad, i2_grad, o2_grad, shares, landing,
     send_sem, recv_sem, own_sem, in_sem, out_sem, share_sem, landing_sem,
 ):
     dp, me = lax.axis_index("dp"), lax.axis_index("mp")
@@ -243,7 +243,7 @@
 
     @pl.loop(0, blocks, unroll=4)
     def _(block):
-        i1_grad[block] = i1_grad[block].T
+        i1_term[block] = i1_grad[block].T.astype(jnp.bfloat16)
 
     for kind in range(4):
         for chunk in range(chunks):
@@ -271,12 +271,12 @@
     in_vmem = pl.BlockSpec(memory_space=pltpu.VMEM)
     anywhere = pl.BlockSpec(memory_space=pl.ANY)
     slab = size // replicas
-    grad = jax.ShapeDtypeStruct((blocks, size, size), jnp.float32)
+    term = jax.ShapeDtypeStruct((blocks, size, size), jnp.bfloat16)
     part = jax.ShapeDtypeStruct((blocks, slab, size), jnp.float32)
     wide = jax.ShapeDtypeStruct((tok_rows + SPARE, width), jnp.bfloat16)
     results = pl.pallas_call(
         functools.partial(monarch_kernel, peers, replicas, chunks, blocks, size),
-        out_shape=(wide, wide, grad, part, part, part),
+        out_shape=(wide, wide, term, part, part, part),
         in_specs=[anywhere] * 2 + [in_vmem] * 4,
         out_specs=(anywhere,) * 2 + (in_vmem,) * 4,
         scratch_shapes=[
@@ -286,7 +286,7 @@
             pltpu.VMEM((4, CHUNK, width), jnp.bfloat16),
             pltpu.VMEM((2, CHUNK, width), jnp.bfloat16),
             *[pltpu.VMEM((blocks, size, size), jnp.bfloat16)] * 3,
-            *[pltpu.VMEM((blocks, size, size), jnp.float32)] * 3,
+            *[pltpu.VMEM((blocks, size, size), jnp.float32)] * 4,
             pltpu.VMEM((3, replicas, blocks, slab, size), jnp.bfloat16),
             pltpu.VMEM((3, replicas, blocks, slab, size), jnp.bfloat16),
             pltpu.SemaphoreType.DMA((4, SLOTS, peers)),
@@ -307,7 +307,9 @@
     )(tokens, cotangent, inner_one, outer_one, inner_two, outer_two)
     output, input_grad, inner_one_term, *sums = results
     inner_one_grad = lax.psum_scatter(inner_one_term, "dp", scatter_dimension=1, tiled=True)
-    return (output[:tok_rows], input_grad[:tok_rows], inner_one_grad, *sums)
+    return (
+        output[:tok_rows], input_grad[:tok_rows], inner_one_grad.astype(jnp.float32), *sums
+    )
 
 
 def gelu_tanh(values):

time: 419 us -> 415 us (level)
  waiting for transfers between devices: 11.2 us -> 5.67 us
    reduce_scatter x1, waiting for transfers between devices: 11.1 us -> 5.65 us  [fused(): lax.psum_scatter(inner_one_term, 'dp', scatter_dimension=1, tiled=True)]
where the time goes in v4:
time: 415 us
  Pallas kernels  375 us (90%)
  local copies, waits for them, and re-layouts  19.1 us (5%)
  between operations  14 us (3%)
  waiting for transfers between devices  5.67 us (1%)
    pallas_call x1, Pallas kernels, fused(): pl.pallas_call(functools.partial(monarch_kernel, peers, replicas, chunks,...  375 us
    slice x1, local copies, waits for them, and re-layouts, fused(): input_grad[:tok_rows]  8.51 us
    slice x1, local copies, waits for them, and re-layouts, fused(): output[:tok_rows]  8.44 us
  transfers between devices with their start and end apart: 1, of which 1 were waited for; matrix products, arithmetic and copies ran while one was open for 4% of the time, Pallas kernels for 0%

profile of v4, /device:TPU:0, one launch (start us, length us, event | category | flops | bytes accessed | tf_op | source)
XLA Modules:
  0.0 415.1 jit_solution(17830356829336567197)
XLA Ops:
  7.2 0.0 reduce-scatter.2.cloned.1.call-start
  7.2 374.6 %shard_map.109 = (bf16[2064,2048]{1,0:T(8,128)(2,1)}, bf16[2064,2048]{1,0:T(8,128)(2,1)}, bf16[16,128,128]{2,1,0:T(8,128)(2,1)}, f32[16,32,128]{2,1,0:T(8,128)},...) custom-call(bf16[2048,2048]{1,0:T(8,128)(2,1)} %x_hbm.1, bf16[2048,2048]{1,0:T(8,128)(2,1)} %g_hbm.1, ...), custom_call_target="tpu_custom_call" | custom-call | flops 12884901888 | bytes 50331648 | tf_op jit(solution)/shard_map/pallas_call | solution.py:277
  381.9 0.0 reduce-scatter.2.cloned.1.call-update
  381.9 8.4 %slice.6 = bf16[2048,2048]{1,0:T(8,128)(2,1)} slice(bf16[2064,2048]{1,0:T(8,128)(2,1)} %get-tuple-element.12), slice={[0:2048], [0:2048]} | slice | bytes 16777216 | tf_op jit(solution)/shard_map/slice | solution.py:311
  390.3 0.0 copy-start.2
  390.3 0.0 copy-start.1
  390.3 0.0 copy-start
  390.3 8.5 %slice.7 = bf16[2048,2048]{1,0:T(8,128)(2,1)} slice(bf16[2064,2048]{1,0:T(8,128)(2,1)} %get-tuple-element.13), slice={[0:2048], [0:2048]} | slice | bytes 16777216 | tf_op jit(solution)/shard_map/slice | solution.py:311
  398.9 5.7 %reduce-scatter.2.cloned.1.call-done = bf16[16,32,128]{2,1,0:T(8,128)(2,1)} async-done(((bf16[16,128,128]{2,1,0:T(8,128)(2,1)}), bf16[16,32,128]{2,1,0:T(8,128)(2,1)}) %reduce-scatter.2.cloned.1.call-update) | async-done | bytes 131088 | tf_op jit(solution)/shard_map/reduce_scatter | solution.py:309
  404.5 1.6 convert_element_type.3
  406.1 0.0 copy-done.2
  406.1 0.7 copy.15
  406.9 0.0 copy-done.1
  406.9 0.7 copy.16
  407.6 0.0 copy-done
  407.6 0.7 copy.17
Async XLA Ops:
  7.2 397.3 %reduce-scatter.2.cloned.1.call-start = ((), (), s32[]{:S(2)}) async-start(), calls=%async_computation.1 | async-start | bytes 655360 | tf_op jit(solution)/shard_map/reduce_scatter | solution.py:309
  390.3 15.8 %copy-start.2 = (f32[16,32,128]{2,1,0:T(8,128)S(1)}, f32[16,32,128]{2,1,0:T(8,128)}, u32[]{:S(2)}) copy-start(f32[16,32,128]{2,1,0:T(8,128)} %get-tuple-element.27) | copy-start | bytes 786436
  390.3 16.5 %copy-start.1 = (f32[16,32,128]{2,1,0:T(8,128)S(1)}, f32[16,32,128]{2,1,0:T(8,128)}, u32[]{:S(2)}) copy-start(f32[16,32,128]{2,1,0:T(8,128)} %get-tuple-element.28) | copy-start | bytes 786436
  390.3 17.2 %copy-start = (f32[16,32,128]{2,1,0:T(8,128)S(1)}, f32[16,32,128]{2,1,0:T(8,128)}, u32[]{:S(2)}) copy-start(f32[16,32,128]{2,1,0:T(8,128)} %get-tuple-element.29) | copy-start | bytes 786436
Sparse Core Ops, SparseCore 0:
  382.0 22.4 reduce-scatter.1
